TPU v7x, 256 devices: a whole 4x4x8 slice. The times are simulated.
256 devices in a mesh: depth: 32 (over x, y, core), tile: 8 (over z).
Axes of the slice: x: 4, y: 4, z: 8, core: 2. Of those that a mesh axis runs over, the one named last changes fastest.
Arguments:
- fronts: float32 [32, 8, 8, 2, 128, 128], P('depth', 'tile'), may hold values from -6 to 6
- probe_wave: float32 [2, 128, 128], replicated, may hold values from -6 to 6
- object_slices: bfloat16 [64, 2, 3072, 384], P('depth', None, 'tile')
- patch_list: int32 [35, 8, 3, 8], P(None, 'tile'), may hold values from 0 to 256, as said below
- counts: int32 [35, 8], P(None, 'tile'), may hold values from 1 to 8, as said below
Outputs:
- exit_waves: float32 [32, 8, 8, 2, 128, 128], P('depth', 'tile')
Inputs may be any that keep to these rules, and one draw needn't show every extreme that they name: `patch_list`: rows and columns of corners run from 0 to 256, and that end is reached. Among the live probes of one batch of one owner no tile is named more than 1 times; a batch of 8 probes names every tile exactly 1 times. `counts`: some batch of some owner holds 8 probes.
All inputs are finite; a program needn't handle non-finite values.
Results may differ from a plain program's by a relative error of at most 0.0003.
Values may be sent and summed in bfloat16 or wider, within the bound.
A program may use at most 64 MiB of HBM per device.

v0:
```python
import math
import jax
import jax.numpy as jnp
from jax import lax
from jax.sharding import PartitionSpec as P

STEPS = 4
fresnel_rate = 0.3


def from_behind(value, axis, steps):
    count = lax.axis_size(axis)
    leading, last = (max(0, -steps), min(count, count - steps))
    return lax.ppermute(value, axis, [(source, source + steps) for source in range(leading, last)])


def dft_tables(width, inverse):
    index = jnp.arange(width, dtype=jnp.int32)
    angle = 2.0 * math.pi / width * (index[:, None] * index[None, :] % width).astype(jnp.float32)
    cosine = jnp.cos(angle)
    sine = jnp.sin(angle)
    if inverse:
        cosine = cosine / width
        imagine = sine / width
    else:
        imagine = -sine
    return (cosine, cosine + imagine, imagine - cosine)


def plane_dot(plane, table):
    shape = plane.shape
    flat = plane.reshape(-1, shape[-1])
    return jnp.dot(
        flat, table, precision=lax.Precision.HIGHEST, preferred_element_type=jnp.float32
    ).reshape(shape)


def right_multiply(real_part, imag_part, tables):
    cosine, summed, differ = tables
    first = plane_dot(real_part + imag_part, cosine)
    second = plane_dot(real_part, differ)
    third = plane_dot(imag_part, summed)
    return (first - third, first + second)


def transform(real_part, imag_part, tables):
    real_part, imag_part = right_multiply(real_part, imag_part, tables)
    return right_multiply(jnp.swapaxes(real_part, -1, -2), jnp.swapaxes(imag_part, -1, -2), tables)


def fresnel(width):
    index = jnp.arange(width, dtype=jnp.int32)
    freq = jnp.where(index < width // 2, index, index - width).astype(jnp.float32)
    phase = -2.0 * math.pi * fresnel_rate / width * (freq[:, None] ** 2 + freq[None, :] ** 2)
    return (jnp.cos(phase), jnp.sin(phase))


def slab_pass(wavefield, patches):
    width = wavefield.shape[-1]
    forward = dft_tables(width, False)
    backward = dft_tables(width, True)
    kernel_cos, kernel_sin = fresnel(width)
    real_part = wavefield[:, 0]
    imag_part = wavefield[:, 1]
    for layer in range(2):
        trans_real = patches[:, layer, 0].astype(jnp.float32)
        trans_imag = patches[:, layer, 1].astype(jnp.float32)
        real_part, imag_part = (
            real_part * trans_real - imag_part * trans_imag,
            real_part * trans_imag + imag_part * trans_real,
        )
        spec_real, spec_imag = transform(real_part, imag_part, forward)
        spec_real, spec_imag = (
            spec_real * kernel_cos - spec_imag * kernel_sin,
            spec_real * kernel_sin + spec_imag * kernel_cos,
        )
        real_part, imag_part = transform(spec_real, spec_imag, backward)
    return jnp.stack([real_part, imag_part], axis=1)


def rank_within(tile_ids, live):
    slot_index = jnp.arange(tile_ids.shape[0], dtype=jnp.int32)
    same = (
        (tile_ids[:, None] == tile_ids[None, :])
        & live[None, :]
        & (slot_index[None, :] < slot_index[:, None])
    )
    return jnp.sum(same.astype(jnp.int32), axis=1)


def cut_from(source, row_value, column_value, width):
    zero = jnp.zeros((), jnp.int32)
    return lax.dynamic_slice(source, (zero, zero, row_value, column_value), (2, 2, width, width))


def per_device(fronts, probe_wave, object_slices, patch_list, counts):
    depth_count = lax.axis_size("depth")
    tile_count = lax.axis_size("tile")
    depth_index = lax.axis_index("depth")
    tile_index = lax.axis_index("tile")
    slots = fronts.shape[2]
    width = fronts.shape[-1]
    pair = slots // tile_count
    slot_index = jnp.arange(slots, dtype=jnp.int32)
    own_lists = patch_list[:, 0]
    own_counts = counts[:, 0]
    batch_ids = [step + depth_count - 1 - depth_index for step in range(STEPS)]
    step_lists = jnp.stack(
        [lax.dynamic_index_in_dim(own_lists, batch, 0, keepdims=False) for batch in batch_ids]
    )
    step_counts = jnp.stack(
        [lax.dynamic_index_in_dim(own_counts, batch, 0, keepdims=False) for batch in batch_ids]
    )

    def outgoing(all_lists, all_counts):
        tile_ids = all_lists[:, 0]
        live = slot_index[None, :] < all_counts[:, None]
        order = jax.vmap(rank_within)(tile_ids, live)
        target = live & (tile_ids == tile_index)
        choose = (
            target[:, None, :]
            & (order[:, None, :] == jnp.arange(pair, dtype=jnp.int32)[None, :, None])
        ).astype(jnp.int32)
        row_start = jnp.sum(choose * all_lists[:, 1][:, None, :], axis=-1)
        column_start = jnp.sum(choose * all_lists[:, 2][:, None, :], axis=-1)
        valid = jnp.sum(choose, axis=-1) > 0

        def cut_local(row_value, column_value):
            return cut_from(object_slices, row_value, column_value, width)

        cuts = jax.vmap(jax.vmap(cut_local))(row_start, column_start)
        return jnp.where(valid[:, :, None, None, None, None], cuts, jnp.zeros_like(cuts))

    wavefield = fronts[0, 0]
    for step in range(STEPS):
        listing = step_lists[step]
        count = step_counts[step]
        live = (slot_index < count).astype(jnp.float32)[:, None, None, None]
        if step > 0:
            arrived = from_behind(wavefield, "depth", 1)
            wavefield = jnp.where(depth_index == 0, probe_wave[None] * live, arrived)
        else:
            wavefield = wavefield * live
        got_lists, got_counts = (
            lax.all_gather(listing[None], "tile", axis=0, tiled=True),
            lax.all_gather(count[None], "tile", axis=0, tiled=True),
        )
        received = lax.all_to_all(
            outgoing(got_lists, got_counts), "tile", split_axis=0, concat_axis=0, tiled=True
        )
        incoming_tile_ids = listing[0]
        incoming_live = slot_index < count
        incoming_order = rank_within(incoming_tile_ids, incoming_live)
        place = incoming_tile_ids * pair + jnp.minimum(incoming_order, pair - 1)
        flat = received.reshape((tile_count * pair,) + received.shape[2:])
        patches = jnp.take(flat, place, axis=0)
        wavefield = slab_pass(wavefield, patches)
    return wavefield[None, None]


def solution(mesh):
    in_specs = (
        P("depth", "tile", None, None, None, None),
        P(),
        P("depth", None, "tile", None),
        P(None, "tile", None, None),
        P(None, "tile"),
    )
    out_specs = P("depth", "tile", None, None, None, None)
    return jax.shard_map(
        per_device, mesh=mesh, in_specs=in_specs, out_specs=out_specs, check_vma=False
    )
```

profile of v0, /device:TPU:38, one launch (start us, length us, event | category | flops | bytes accessed | tf_op | source)
XLA Modules:
  0.0 397.6 jit_solution(2629929279038056412)
XLA Ops:
  1.3 1.5 constant_dynamic-slice_fusion.9
  5.3 1.4 bitcast_dynamic-update-slice_fusion.6
  7.9 15.2 %all-reduce.4 = (s32[8]{0:T(128)S(1)}, s32[8]{0:T(128)S(1)}, s32[8]{0:T(128)S(1)}, s32[8]{0:T(128)S(1)}) all-reduce(s32[8]{0:T(128)S(1)} %bitcast_dynamic-update-slice_fusion.4, s32[8]{0:T(128)S(1)} %bitcast_dynamic-update-slice_fusion.5, s32[8]{0:T(128)S(1)} %bitcast_dynamic-update-slice_fusion.6, ...), channel_id=8, replica_groups=mesh['depth'=32,'tile'=8] {'tile'}, use_global_device_ids=true, to_apply=%add.3 | all-reduce | flops 32 | bytes 256 | tf_op jit(solution)/shard_map/all_gather | solution.py:146
  24.5 20.8 %all-gather.7 = s32[8,1,3,8]{3,1,2,0:T(1,128)S(1)} all-gather(s32[1,1,3,8]{3,1,2,0:T(1,128)S(1)} %copy.293), channel_id=9, replica_groups=mesh['depth'=32,'tile'=8] {'tile'}, dimensions={0}, use_global_device_ids=true | all-gather | bytes 864 | tf_op jit(solution)/shard_map/all_gather | solution.py:145
  45.4 20.7 %all-gather.5 = s32[8,1,3,8]{3,1,2,0:T(1,128)S(1)} all-gather(s32[1,1,3,8]{3,1,2,0:T(1,128)S(1)} %copy.292), channel_id=7, replica_groups=mesh['depth'=32,'tile'=8] {'tile'}, dimensions={0}, use_global_device_ids=true | all-gather | bytes 864 | tf_op jit(solution)/shard_map/all_gather | solution.py:145
  66.2 20.7 %all-gather.3 = s32[8,1,3,8]{3,1,2,0:T(1,128)S(1)} all-gather(s32[1,1,3,8]{3,1,2,0:T(1,128)S(1)} %copy.291), channel_id=5, replica_groups=mesh['depth'=32,'tile'=8] {'tile'}, dimensions={0}, use_global_device_ids=true | all-gather | bytes 864 | tf_op jit(solution)/shard_map/all_gather | solution.py:145
  87.0 21.1 %all-gather.1 = s32[8,1,3,8]{3,1,2,0:T(1,128)S(1)} all-gather(s32[1,1,3,8]{3,1,2,0:T(1,128)S(1)} %copy.290), channel_id=3, replica_groups=mesh['depth'=32,'tile'=8] {'tile'}, dimensions={0}, use_global_device_ids=true | all-gather | bytes 864 | tf_op jit(solution)/shard_map/all_gather | solution.py:145
  110.1 24.6 %while.4 = (s32[]{:T(128)}, bf16[2,2,384,384]{3,2,1,0:T(8,128)(2,1)}, s32[8,4]{0,1:T(4,128)S(1)}, bf16[8,2,2,128,128]{4,3,2,1,0:T(8,128)(2,1)S(1)}, s32[]{:T(128)}) while((s32[]{:T(128)}, bf16[2,2,384,384]{3,2,1,0:T(8,128)(2,1)}, s32[8,4]{0,1:T(4,128)S(1)}, bf16[8,2,2,128,128]{4,3,2,1,0:T(8,128)(2,1)S(1)}, s32[]{:T(128)}) %tuple.93), condition=%wide.while_cond, body=%wide.while_body.sunk | while | flops 2 | bytes 262269 | solution.py:93
  110.8 2.4 bitcast_dynamic-update-slice_fusion.12
  113.9 2.4 bitcast_dynamic-update-slice_fusion.12
  116.9 2.4 bitcast_dynamic-update-slice_fusion.12
  120.0 2.4 bitcast_dynamic-update-slice_fusion.12
  123.1 2.4 bitcast_dynamic-update-slice_fusion.12
  126.2 2.4 bitcast_dynamic-update-slice_fusion.12
  129.2 2.4 bitcast_dynamic-update-slice_fusion.12
  132.3 2.4 bitcast_dynamic-update-slice_fusion.12
  135.9 6.2 %all-to-all-start = ((bf16[8,1,2,2,128,128]{5,4,3,2,1,0:T(8,128)(2,1)}), bf16[8,1,2,2,128,128]{5,4,3,2,1,0:T(8,128)(2,1)S(1)}, u32[]{:S(2)}, u32[]{:S(2)}) async-start(bf16[8,1,2,2,128,128]{5,4,3,2,1,0:T(8,128)(2,1)} %bitcast_select_fusion.3), calls=%async_computation | async-start | bytes 2097152 | tf_op jit(solution)/shard_map/all_to_all | solution.py:148
  145.4 24.1 %while.5 = (s32[]{:T(128)}, bf16[2,2,384,384]{3,2,1,0:T(8,128)(2,1)}, s32[8,4]{0,1:T(4,128)S(1)}, bf16[8,2,2,128,128]{4,3,2,1,0:T(8,128)(2,1)S(1)}, s32[]{:T(128)}) while((s32[]{:T(128)}, bf16[2,2,384,384]{3,2,1,0:T(8,128)(2,1)}, s32[8,4]{0,1:T(4,128)S(1)}, bf16[8,2,2,128,128]{4,3,2,1,0:T(8,128)(2,1)S(1)}, s32[]{:T(128)}) %tuple.105), condition=%wide.while_cond.1, body=%wide.while_body.1.sunk | while | flops 2 | bytes 262269 | solution.py:93
  146.1 2.3 bitcast_dynamic-update-slice_fusion.13
  149.1 2.3 bitcast_dynamic-update-slice_fusion.13
  152.1 2.3 bitcast_dynamic-update-slice_fusion.13
  155.1 2.3 bitcast_dynamic-update-slice_fusion.13
  158.1 2.3 bitcast_dynamic-update-slice_fusion.13
  161.1 2.3 bitcast_dynamic-update-slice_fusion.13
  164.1 2.3 bitcast_dynamic-update-slice_fusion.13
  167.1 2.3 bitcast_dynamic-update-slice_fusion.13
  171.6 29.4 %while.6 = (s32[]{:T(128)}, bf16[2,2,384,384]{3,2,1,0:T(8,128)(2,1)}, s32[8,4]{0,1:T(4,128)S(1)}, bf16[8,2,2,128,128]{4,3,2,1,0:T(8,128)(2,1)}, s32[]{:T(128)}) while((s32[]{:T(128)}, bf16[2,2,384,384]{3,2,1,0:T(8,128)(2,1)}, s32[8,4]{0,1:T(4,128)S(1)}, bf16[8,2,2,128,128]{4,3,2,1,0:T(8,128)(2,1)}, s32[]{:T(128)}) %tuple.106), condition=%wide.while_cond.2, body=%wide.while_body.2.sunk | while | flops 2 | bytes 263793 | solution.py:93
  172.2 3.0 bitcast_dynamic-update-slice_fusion.14
  175.9 3.0 bitcast_dynamic-update-slice_fusion.14
  179.6 3.0 bitcast_dynamic-update-slice_fusion.14
  183.3 3.0 bitcast_dynamic-update-slice_fusion.14
  186.9 3.0 bitcast_dynamic-update-slice_fusion.14
  190.6 3.0 bitcast_dynamic-update-slice_fusion.14
  194.3 3.0 bitcast_dynamic-update-slice_fusion.14
  198.0 3.0 bitcast_dynamic-update-slice_fusion.14
  201.0 1.4 bitcast_multiply_fusion
  203.8 23.7 %while.7 = (s32[]{:T(128)}, bf16[2,2,384,384]{3,2,1,0:T(8,128)(2,1)}, s32[8,4]{0,1:T(4,128)S(1)}, bf16[8,2,2,128,128]{4,3,2,1,0:T(8,128)(2,1)S(1)}, s32[]{:T(128)}) while((s32[]{:T(128)}, bf16[2,2,384,384]{3,2,1,0:T(8,128)(2,1)}, s32[8,4]{0,1:T(4,128)S(1)}, bf16[8,2,2,128,128]{4,3,2,1,0:T(8,128)(2,1)S(1)}, s32[]{:T(128)}) %tuple.107), condition=%wide.while_cond.3, body=%wide.while_body.3.sunk | while | flops 2 | bytes 262269 | solution.py:93
  204.4 2.3 bitcast_dynamic-update-slice_fusion.15
  207.4 2.3 bitcast_dynamic-update-slice_fusion.15
  210.3 2.3 bitcast_dynamic-update-slice_fusion.15
  213.3 2.3 bitcast_dynamic-update-slice_fusion.15
  216.3 2.3 bitcast_dynamic-update-slice_fusion.15
  219.2 2.3 bitcast_dynamic-update-slice_fusion.15
  222.2 2.3 bitcast_dynamic-update-slice_fusion.15
  225.2 2.3 bitcast_dynamic-update-slice_fusion.15
  227.5 7.4 %all-to-all-start.1 = ((bf16[8,1,2,2,128,128]{5,4,3,2,1,0:T(8,128)(2,1)}), bf16[8,1,2,2,128,128]{5,4,3,2,1,0:T(8,128)(2,1)}, u32[]{:S(2)}, u32[]{:S(2)}) async-start(bf16[8,1,2,2,128,128]{5,4,3,2,1,0:T(8,128)(2,1)} %bitcast_select_fusion.2), calls=%async_computation.1 | async-start | bytes 2097152 | tf_op jit(solution)/shard_map/all_to_all | solution.py:148
  246.9 1.6 convolution_subtract_fusion.28
  258.4 1.3 fusion.31
  261.0 1.9 collective-permute-start
  263.6 2.3 bitcast_select_fusion.1
  266.0 7.2 %all-to-all-start.2 = ((bf16[8,1,2,2,128,128]{5,4,3,2,1,0:T(8,128)(2,1)}), bf16[8,1,2,2,128,128]{5,4,3,2,1,0:T(8,128)(2,1)S(1)}, u32[]{:S(2)}, u32[]{:S(2)}) async-start(bf16[8,1,2,2,128,128]{5,4,3,2,1,0:T(8,128)(2,1)} %bitcast_select_fusion.1), calls=%async_computation.2 | async-start | bytes 2097152 | tf_op jit(solution)/shard_map/all_to_all | solution.py:148
  273.2 2.0 gather_fusion.1
  275.3 4.0 %collective-permute-done = f32[8,2,128,128]{3,2,0,1:T(8,128)} collective-permute-done((f32[8,2,128,128]{3,2,0,1:T(8,128)S(1)}, f32[8,2,128,128]{3,2,0,1:T(8,128)}, u32[]{:S(2)}, u32[]{:S(2)}) %collective-permute-start) | collective-permute-done | bytes 1048608 | tf_op jit(solution)/shard_map/ppermute | solution.py:14
  279.4 1.4 multiply_select_fusion
  291.9 1.6 convolution_subtract_fusion.20
  303.4 1.3 fusion.21
  306.9 1.9 collective-permute-start.1
  310.8 7.2 %all-to-all-start.3 = ((bf16[8,1,2,2,128,128]{5,4,3,2,1,0:T(8,128)(2,1)}), bf16[8,1,2,2,128,128]{5,4,3,2,1,0:T(8,128)(2,1)S(1)}, u32[]{:S(2)}, u32[]{:S(2)}) async-start(bf16[8,1,2,2,128,128]{5,4,3,2,1,0:T(8,128)(2,1)} %bitcast_select_fusion), calls=%async_computation.3 | async-start | bytes 2097152 | tf_op jit(solution)/shard_map/all_to_all | solution.py:148
  318.9 6.5 %collective-permute-done.1 = f32[8,2,128,128]{3,2,0,1:T(8,128)} collective-permute-done((f32[8,2,128,128]{3,2,0,1:T(8,128)}, f32[8,2,128,128]{3,2,0,1:T(8,128)}, u32[]{:S(2)}, u32[]{:S(2)}) %collective-permute-start.1) | collective-permute-done | bytes 1048608 | tf_op jit(solution)/shard_map/ppermute | solution.py:14
  325.4 1.4 multiply_select_fusion.1
  337.9 1.6 convolution_subtract_fusion.12
  352.9 1.9 collective-permute-start.2
  356.6 14.8 %collective-permute-done.2 = f32[8,2,128,128]{3,2,0,1:T(8,128)S(1)} collective-permute-done((f32[8,2,128,128]{3,2,0,1:T(8,128)}, f32[8,2,128,128]{3,2,0,1:T(8,128)S(1)}, u32[]{:S(2)}, u32[]{:S(2)}) %collective-permute-start.2) | collective-permute-done | bytes 1048608 | tf_op jit(solution)/shard_map/ppermute | solution.py:14
  382.6 1.4 convolution_subtract_fusion.4
  (250 shorter events, 137.3 us)
Async XLA Ops:
  135.9 91.7 %all-to-all-start = ((bf16[8,1,2,2,128,128]{5,4,3,2,1,0:T(8,128)(2,1)}), bf16[8,1,2,2,128,128]{5,4,3,2,1,0:T(8,128)(2,1)S(1)}, u32[]{:S(2)}, u32[]{:S(2)}) async-start(bf16[8,1,2,2,128,128]{5,4,3,2,1,0:T(8,128)(2,1)} %bitcast_select_fusion.3), calls=%async_computation | async-start | bytes 2097152 | tf_op jit(solution)/shard_map/all_to_all | solution.py:148
  227.5 7.4 %copy-start = (bf16[8,2,2,128,128]{4,3,2,1,0:T(8,128)(2,1)}, bf16[8,2,2,128,128]{4,3,2,1,0:T(8,128)(2,1)S(1)}, u32[]{:S(2)}) copy-start(bf16[8,2,2,128,128]{4,3,2,1,0:T(8,128)(2,1)S(1)} %get-tuple-element.37) | copy-start | bytes 3145732
  227.5 38.4 %all-to-all-start.1 = ((bf16[8,1,2,2,128,128]{5,4,3,2,1,0:T(8,128)(2,1)}), bf16[8,1,2,2,128,128]{5,4,3,2,1,0:T(8,128)(2,1)}, u32[]{:S(2)}, u32[]{:S(2)}) async-start(bf16[8,1,2,2,128,128]{5,4,3,2,1,0:T(8,128)(2,1)} %bitcast_select_fusion.2), calls=%async_computation.1 | async-start | bytes 2097152 | tf_op jit(solution)/shard_map/all_to_all | solution.py:148
  261.0 18.3 %collective-permute-start = (f32[8,2,128,128]{3,2,0,1:T(8,128)S(1)}, f32[8,2,128,128]{3,2,0,1:T(8,128)}, u32[]{:S(2)}, u32[]{:S(2)}) collective-permute-start(f32[8,2,128,128]{3,2,0,1:T(8,128)S(1)} %pad_maximum_fusion), channel_id=1, source_target_pairs={{0,8},{8,16},{16,24},{24,32},{32,40},{40,48},{48,56},{56,64},{64,7... | collective-permute-start | bytes 3145736 | tf_op jit(solution)/shard_map/ppermute | solution.py:14
  266.0 44.8 %all-to-all-start.2 = ((bf16[8,1,2,2,128,128]{5,4,3,2,1,0:T(8,128)(2,1)}), bf16[8,1,2,2,128,128]{5,4,3,2,1,0:T(8,128)(2,1)S(1)}, u32[]{:S(2)}, u32[]{:S(2)}) async-start(bf16[8,1,2,2,128,128]{5,4,3,2,1,0:T(8,128)(2,1)} %bitcast_select_fusion.1), calls=%async_computation.2 | async-start | bytes 2097152 | tf_op jit(solution)/shard_map/all_to_all | solution.py:148
  275.1 4.2 %copy-start.2 = (f32[2,128,128]{2,1,0:T(8,128)S(1)}, f32[2,128,128]{2,1,0:T(8,128)}, u32[]{:S(2)}) copy-start(f32[2,128,128]{2,1,0:T(8,128)} %param.8) | copy-start | bytes 393220
  305.9 3.8 copy-start.1
  306.9 18.5 %collective-permute-start.1 = (f32[8,2,128,128]{3,2,0,1:T(8,128)}, f32[8,2,128,128]{3,2,0,1:T(8,128)}, u32[]{:S(2)}, u32[]{:S(2)}) collective-permute-start(f32[8,2,128,128]{3,2,0,1:T(8,128)} %pad_maximum_fusion.1), channel_id=1, source_target_pairs={{0,8},{8,16},{16,24},{24,32},{32,40},{40,48},{48,56},{56,64},{64,7... | collective-permute-start | bytes 3145736 | tf_op jit(solution)/shard_map/ppermute | solution.py:14
  310.8 44.9 %all-to-all-start.3 = ((bf16[8,1,2,2,128,128]{5,4,3,2,1,0:T(8,128)(2,1)}), bf16[8,1,2,2,128,128]{5,4,3,2,1,0:T(8,128)(2,1)S(1)}, u32[]{:S(2)}, u32[]{:S(2)}) async-start(bf16[8,1,2,2,128,128]{5,4,3,2,1,0:T(8,128)(2,1)} %bitcast_select_fusion), calls=%async_computation.3 | async-start | bytes 2097152 | tf_op jit(solution)/shard_map/all_to_all | solution.py:148
  352.9 18.4 %collective-permute-start.2 = (f32[8,2,128,128]{3,2,0,1:T(8,128)}, f32[8,2,128,128]{3,2,0,1:T(8,128)S(1)}, u32[]{:S(2)}, u32[]{:S(2)}) collective-permute-start(f32[8,2,128,128]{3,2,0,1:T(8,128)} %pad_maximum_fusion.2), channel_id=1, source_target_pairs={{0,8},{8,16},{16,24},{24,32},{32,40},{40,48},{48,56},{56,64},{64,7... | collective-permute-start | bytes 3145736 | tf_op jit(solution)/shard_map/ppermute | solution.py:14
where the time goes:
time: 404 us; the launch traced here: 398 us
  local copies, waits for them, and re-layouts  118 us (29%)
  matrix products  99.2 us (25%)
  blocking collectives  98.6 us (24%)
  starting transfers between devices  33.7 us (8%)
  waiting for transfers between devices  25.3 us (6%)
  other arithmetic  21 us (5%)
    gather x96, local copies, waits for them, and re-layouts  101 us
    dot_general x96, matrix products, plane_dot(): jnp.dot(flat, table, precision=lax.Precision.HIGHEST, preferred_element_t...  99.2 us
    all_gather x4, blocking collectives, per_device(): lax.all_gather(listing[None], 'tile', axis=0, tiled=True)  83.4 us
    all_to_all x4, starting transfers between devices, per_device(): lax.all_to_all(outgoing(got_lists, got_counts), 'tile', split_axis=0, con...  28 us
    ppermute x3, waiting for transfers between devices, from_behind(): lax.ppermute(value, axis, [(source, source + steps) for source in range(l...  25.3 us
    all_gather x1, blocking collectives, per_device(): lax.all_gather(count[None], 'tile', axis=0, tiled=True)  15.2 us
    unnamed x23, local copies, waits for them, and re-layouts  8.72 us
  transfers between devices with their start and end apart: 7, of which 3 were waited for; matrix products, arithmetic and copies ran while one was open for 44% of the time, Pallas kernels for 0%

commit v1 on v0

--- a/solution.py
+++ b/solution.py
@@ -141,8 +141,16 @@
             wavefield = jnp.where(depth_index == 0, probe_wave[None] * live, arrived)
         else:
             wavefield = wavefield * live
+
+        def raise_plane(unit):
+            spare = jnp.concatenate([unit for _ in range(lax.psum(1, axis_name="tile"))], 0)
+            mat_out = lax.all_to_all(
+                spare, axis_name="tile", split_axis=0, concat_axis=0, tiled=True
+            )
+            return mat_out
+
         got_lists, got_counts = (
-            lax.all_gather(listing[None], "tile", axis=0, tiled=True),
+            raise_plane(listing[None]),
             lax.all_gather(count[None], "tile", axis=0, tiled=True),
         )
         received = lax.all_to_all(

time: 404 us -> 347 us (0.86)
  blocking collectives: 98.6 us -> 12.6 us
  starting transfers between devices: 33.7 us -> 56.5 us
  waiting for transfers between devices: 25.3 us -> 34 us
    all_gather x4 -> x0, blocking collectives: 83.4 us -> none  [per_device(): lax.all_gather(listing[None], 'tile', axis=0, tiled=True)]
    all_to_all x0 -> x4, starting transfers between devices: none -> 23 us  [raise_plane(): lax.all_to_all(spare, axis_name='tile', split_axis=0, concat_axis=0, tile...]
    all_to_all x0 -> x4, waiting for transfers between devices: none -> 19.1 us  [raise_plane(): lax.all_to_all(spare, axis_name='tile', split_axis=0, concat_axis=0, tile...]
    ppermute x3, waiting for transfers between devices: 25.3 us -> 14.9 us  [from_behind(): lax.ppermute(value, axis, [(source, source + steps) for source in range(l...]
    gather x96, local copies, waits for them, and re-layouts: 101 us -> 96.6 us
    unnamed x23 -> x17, local copies, waits for them, and re-layouts: 8.72 us -> 7.89 us
  transfers between devices with their start and end apart: 7 -> 11, of which waited for: 3 -> 4; matrix products, arithmetic and copies ran while one was open for 44% -> 52% of each run, Pallas kernels for 0% -> 0%
where the time goes in v1:
time: 347 us; the launch traced here: 341 us
  local copies, waits for them, and re-layouts  116 us (33%)
  matrix products  99.2 us (29%)
  starting transfers between devices  56.5 us (16%)
  waiting for transfers between devices  34 us (10%)
  other arithmetic  20.3 us (6%)
  blocking collectives  12.6 us (4%)
    dot_general x96, matrix products, plane_dot(): jnp.dot(flat, table, precision=lax.Precision.HIGHEST, preferred_element_t...  99.2 us
    gather x96, local copies, waits for them, and re-layouts  96.6 us
    all_to_all x4, starting transfers between devices, per_device(): lax.all_to_all(outgoing(got_lists, got_counts), 'tile', split_axis=0, con...  26.7 us
    all_to_all x4, starting transfers between devices, raise_plane(): lax.all_to_all(spare, axis_name='tile', split_axis=0, concat_axis=0, tile...  23 us
    all_to_all x4, waiting for transfers between devices, raise_plane(): lax.all_to_all(spare, axis_name='tile', split_axis=0, concat_axis=0, tile...  19.1 us
    ppermute x3, waiting for transfers between devices, from_behind(): lax.ppermute(value, axis, [(source, source + steps) for source in range(l...  14.9 us
    all_gather x1, blocking collectives, per_device(): lax.all_gather(count[None], 'tile', axis=0, tiled=True)  12.6 us
    unnamed x17, local copies, waits for them, and re-layouts  7.89 us
  transfers between devices with their start and end apart: 11, of which 4 were waited for; matrix products, arithmetic and copies ran while one was open for 52% of the time, Pallas kernels for 0%

profile of v1, /device:TPU:38, one launch (start us, length us, event | category | flops | bytes accessed | tf_op | source)
XLA Modules:
  0.0 340.6 jit_solution(9757497156792930265)
XLA Ops:
  1.8 8.6 %all-to-all-start.2 = ((s32[8,3,8]{2,1,0:T(4,128)}), s32[8,3,8]{2,1,0:T(4,128)S(1)}, u32[]{:S(2)}, u32[]{:S(2)}) async-start(s32[8,3,8]{2,1,0:T(4,128)} %concatenate.26), calls=%async_computation.2 | async-start | bytes 32768 | tf_op jit(solution)/shard_map/all_to_all | solution.py:147
  10.4 1.5 constant_dynamic-slice_fusion.5
  21.7 12.6 %all-reduce.4 = (s32[8]{0:T(128)S(1)}, s32[8]{0:T(128)S(1)}, s32[8]{0:T(128)S(1)}, s32[8]{0:T(128)S(1)}) all-reduce(s32[8]{0:T(128)S(1)} %bitcast_dynamic-update-slice_fusion.4, s32[8]{0:T(128)S(1)} %bitcast_dynamic-update-slice_fusion.5, s32[8]{0:T(128)S(1)} %bitcast_dynamic-update-slice_fusion.6, ...), channel_id=5, replica_groups=mesh['depth'=32,'tile'=8] {'tile'}, use_global_device_ids=true, to_apply=%add.3 | all-reduce | flops 32 | bytes 256 | tf_op jit(solution)/shard_map/all_gather | solution.py:154
  36.6 1.4 bitcast_multiply_fusion
  39.4 5.1 %all-to-all-start.4 = ((s32[8,3,8]{2,1,0:T(4,128)}), s32[8,3,8]{2,1,0:T(4,128)S(1)}, u32[]{:S(2)}, u32[]{:S(2)}) async-start(s32[8,3,8]{2,1,0:T(4,128)} %concatenate.28), calls=%async_computation.4 | async-start | bytes 32768 | tf_op jit(solution)/shard_map/all_to_all | solution.py:147
  44.5 6.4 %all-to-all-done.4 = s32[8,3,8]{2,1,0:T(4,128)S(1)} async-done(((s32[8,3,8]{2,1,0:T(4,128)}), s32[8,3,8]{2,1,0:T(4,128)S(1)}, u32[]{:S(2)}, u32[]{:S(2)}) %all-to-all-start.4) | async-done | bytes 800 | tf_op jit(solution)/shard_map/all_to_all | solution.py:147
  51.4 4.7 %all-to-all-start = ((s32[8,3,8]{2,1,0:T(4,128)}), s32[8,3,8]{2,1,0:T(4,128)S(1)}, u32[]{:S(2)}, u32[]{:S(2)}) async-start(s32[8,3,8]{2,1,0:T(4,128)} %concatenate.24), calls=%async_computation | async-start | bytes 32768 | tf_op jit(solution)/shard_map/all_to_all | solution.py:147
  56.1 6.4 %all-to-all-done = s32[8,3,8]{2,1,0:T(4,128)S(1)} async-done(((s32[8,3,8]{2,1,0:T(4,128)}), s32[8,3,8]{2,1,0:T(4,128)S(1)}, u32[]{:S(2)}, u32[]{:S(2)}) %all-to-all-start) | async-done | bytes 800 | tf_op jit(solution)/shard_map/all_to_all | solution.py:147
  63.1 4.7 %all-to-all-start.6 = ((s32[8,3,8]{2,1,0:T(4,128)}), s32[8,3,8]{2,1,0:T(4,128)S(1)}, u32[]{:S(2)}, u32[]{:S(2)}) async-start(s32[8,3,8]{2,1,0:T(4,128)} %concatenate.30), calls=%async_computation.6 | async-start | bytes 32768 | tf_op jit(solution)/shard_map/all_to_all | solution.py:147
  67.8 6.4 %all-to-all-done.6 = s32[8,3,8]{2,1,0:T(4,128)S(1)} async-done(((s32[8,3,8]{2,1,0:T(4,128)}), s32[8,3,8]{2,1,0:T(4,128)S(1)}, u32[]{:S(2)}, u32[]{:S(2)}) %all-to-all-start.6) | async-done | bytes 800 | tf_op jit(solution)/shard_map/all_to_all | solution.py:147
  75.7 24.7 %while.4 = (s32[]{:T(128)}, bf16[2,2,384,384]{3,2,1,0:T(8,128)(2,1)}, s32[8,4]{0,1:T(4,128)S(1)}, bf16[8,2,2,128,128]{4,3,2,1,0:T(8,128)(2,1)S(1)}, s32[]{:T(128)}) while((s32[]{:T(128)}, bf16[2,2,384,384]{3,2,1,0:T(8,128)(2,1)}, s32[8,4]{0,1:T(4,128)S(1)}, bf16[8,2,2,128,128]{4,3,2,1,0:T(8,128)(2,1)S(1)}, s32[]{:T(128)}) %tuple.106), condition=%wide.while_cond, body=%wide.while_body.sunk | while | flops 2 | bytes 262269 | solution.py:93
  76.4 2.4 bitcast_dynamic-update-slice_fusion.12
  79.5 2.4 bitcast_dynamic-update-slice_fusion.12
  82.6 2.4 bitcast_dynamic-update-slice_fusion.12
  85.7 2.4 bitcast_dynamic-update-slice_fusion.12
  88.8 2.4 bitcast_dynamic-update-slice_fusion.12
  91.9 2.4 bitcast_dynamic-update-slice_fusion.12
  95.0 2.4 bitcast_dynamic-update-slice_fusion.12
  98.0 2.4 bitcast_dynamic-update-slice_fusion.12
  101.6 4.9 %all-to-all-start.1 = ((bf16[8,1,2,2,128,128]{5,4,3,2,1,0:T(8,128)(2,1)}), bf16[8,1,2,2,128,128]{5,4,3,2,1,0:T(8,128)(2,1)S(1)}, u32[]{:S(2)}, u32[]{:S(2)}) async-start(bf16[8,1,2,2,128,128]{5,4,3,2,1,0:T(8,128)(2,1)} %bitcast_select_fusion.3), calls=%async_computation.1 | async-start | bytes 2097152 | tf_op jit(solution)/shard_map/all_to_all | solution.py:156
  106.7 24.6 %while.5 = (s32[]{:T(128)}, bf16[2,2,384,384]{3,2,1,0:T(8,128)(2,1)}, s32[8,4]{0,1:T(4,128)S(1)}, bf16[8,2,2,128,128]{4,3,2,1,0:T(8,128)(2,1)S(1)}, s32[]{:T(128)}) while((s32[]{:T(128)}, bf16[2,2,384,384]{3,2,1,0:T(8,128)(2,1)}, s32[8,4]{0,1:T(4,128)S(1)}, bf16[8,2,2,128,128]{4,3,2,1,0:T(8,128)(2,1)S(1)}, s32[]{:T(128)}) %tuple.118), condition=%wide.while_cond.1, body=%wide.while_body.1.sunk | while | flops 2 | bytes 262269 | solution.py:93
  107.4 2.4 bitcast_dynamic-update-slice_fusion.13
  110.5 2.4 bitcast_dynamic-update-slice_fusion.13
  113.5 2.4 bitcast_dynamic-update-slice_fusion.13
  116.6 2.4 bitcast_dynamic-update-slice_fusion.13
  119.7 2.4 bitcast_dynamic-update-slice_fusion.13
  122.8 2.4 bitcast_dynamic-update-slice_fusion.13
  125.9 2.4 bitcast_dynamic-update-slice_fusion.13
  128.9 2.4 bitcast_dynamic-update-slice_fusion.13
  132.5 7.4 %all-to-all-start.3 = ((bf16[8,1,2,2,128,128]{5,4,3,2,1,0:T(8,128)(2,1)}), bf16[8,1,2,2,128,128]{5,4,3,2,1,0:T(8,128)(2,1)S(1)}, u32[]{:S(2)}, u32[]{:S(2)}) async-start(bf16[8,1,2,2,128,128]{5,4,3,2,1,0:T(8,128)(2,1)} %bitcast_select_fusion.2), calls=%async_computation.3 | async-start | bytes 2097152 | tf_op jit(solution)/shard_map/all_to_all | solution.py:156
  139.9 2.0 gather_fusion
  153.1 1.6 convolution_subtract_fusion.28
  164.6 1.3 fusion.31
  168.2 1.9 collective-permute-start
  170.3 23.7 %while.6 = (s32[]{:T(128)}, bf16[2,2,384,384]{3,2,1,0:T(8,128)(2,1)}, s32[8,4]{0,1:T(4,128)S(1)}, bf16[8,2,2,128,128]{4,3,2,1,0:T(8,128)(2,1)S(1)}, s32[]{:T(128)}) while((s32[]{:T(128)}, bf16[2,2,384,384]{3,2,1,0:T(8,128)(2,1)}, s32[8,4]{0,1:T(4,128)S(1)}, bf16[8,2,2,128,128]{4,3,2,1,0:T(8,128)(2,1)S(1)}, s32[]{:T(128)}) %tuple.119), condition=%wide.while_cond.2, body=%wide.while_body.2.sunk | while | flops 2 | bytes 262269 | solution.py:93
  170.9 2.3 bitcast_dynamic-update-slice_fusion.14
  173.9 2.3 bitcast_dynamic-update-slice_fusion.14
  176.9 2.3 bitcast_dynamic-update-slice_fusion.14
  179.8 2.3 bitcast_dynamic-update-slice_fusion.14
  182.8 2.3 bitcast_dynamic-update-slice_fusion.14
  185.8 2.3 bitcast_dynamic-update-slice_fusion.14
  188.7 2.3 bitcast_dynamic-update-slice_fusion.14
  191.7 2.3 bitcast_dynamic-update-slice_fusion.14
  195.2 7.2 %all-to-all-start.5 = ((bf16[8,1,2,2,128,128]{5,4,3,2,1,0:T(8,128)(2,1)}), bf16[8,1,2,2,128,128]{5,4,3,2,1,0:T(8,128)(2,1)S(1)}, u32[]{:S(2)}, u32[]{:S(2)}) async-start(bf16[8,1,2,2,128,128]{5,4,3,2,1,0:T(8,128)(2,1)} %bitcast_select_fusion.1), calls=%async_computation.5 | async-start | bytes 2097152 | tf_op jit(solution)/shard_map/all_to_all | solution.py:156
  204.1 1.4 multiply_select_fusion
  216.6 1.6 convolution_subtract_fusion.20
  228.1 1.3 fusion.21
  231.6 3.0 collective-permute-start.1
  234.9 24.0 %while.7 = (s32[]{:T(128)}, bf16[2,2,384,384]{3,2,1,0:T(8,128)(2,1)}, s32[8,4]{0,1:T(4,128)S(1)}, bf16[8,2,2,128,128]{4,3,2,1,0:T(8,128)(2,1)S(1)}, s32[]{:T(128)}) while((s32[]{:T(128)}, bf16[2,2,384,384]{3,2,1,0:T(8,128)(2,1)}, s32[8,4]{0,1:T(4,128)S(1)}, bf16[8,2,2,128,128]{4,3,2,1,0:T(8,128)(2,1)S(1)}, s32[]{:T(128)}) %tuple.120), condition=%wide.while_cond.3, body=%wide.while_body.3.sunk | while | flops 2 | bytes 262269 | solution.py:93
  235.5 2.4 bitcast_dynamic-update-slice_fusion.15
  238.5 2.4 bitcast_dynamic-update-slice_fusion.15
  241.5 2.4 bitcast_dynamic-update-slice_fusion.15
  244.5 2.4 bitcast_dynamic-update-slice_fusion.15
  247.5 2.4 bitcast_dynamic-update-slice_fusion.15
  250.5 2.4 bitcast_dynamic-update-slice_fusion.15
  253.5 2.4 bitcast_dynamic-update-slice_fusion.15
  256.5 2.4 bitcast_dynamic-update-slice_fusion.15
  260.0 7.2 %all-to-all-start.7 = ((bf16[8,1,2,2,128,128]{5,4,3,2,1,0:T(8,128)(2,1)}), bf16[8,1,2,2,128,128]{5,4,3,2,1,0:T(8,128)(2,1)S(1)}, u32[]{:S(2)}, u32[]{:S(2)}) async-start(bf16[8,1,2,2,128,128]{5,4,3,2,1,0:T(8,128)(2,1)} %bitcast_select_fusion), calls=%async_computation.7 | async-start | bytes 2097152 | tf_op jit(solution)/shard_map/all_to_all | solution.py:156
  268.2 1.4 multiply_select_fusion.1
  280.7 1.6 convolution_subtract_fusion.12
  294.8 1.9 collective-permute-start.2
  298.2 14.9 %collective-permute-done.2 = f32[8,2,128,128]{3,2,0,1:T(8,128)} collective-permute-done((f32[8,2,128,128]{3,2,0,1:T(8,128)S(1)}, f32[8,2,128,128]{3,2,0,1:T(8,128)}, u32[]{:S(2)}, u32[]{:S(2)}) %collective-permute-start.2) | collective-permute-done | bytes 1048608 | tf_op jit(solution)/shard_map/ppermute | solution.py:14
  313.1 1.4 multiply_select_fusion.2
  325.6 1.4 convolution_subtract_fusion.4
  (247 shorter events, 141.7 us)
Async XLA Ops:
  1.8 36.9 %all-to-all-start.2 = ((s32[8,3,8]{2,1,0:T(4,128)}), s32[8,3,8]{2,1,0:T(4,128)S(1)}, u32[]{:S(2)}, u32[]{:S(2)}) async-start(s32[8,3,8]{2,1,0:T(4,128)} %concatenate.26), calls=%async_computation.2 | async-start | bytes 32768 | tf_op jit(solution)/shard_map/all_to_all | solution.py:147
  39.4 11.5 %all-to-all-start.4 = ((s32[8,3,8]{2,1,0:T(4,128)}), s32[8,3,8]{2,1,0:T(4,128)S(1)}, u32[]{:S(2)}, u32[]{:S(2)}) async-start(s32[8,3,8]{2,1,0:T(4,128)} %concatenate.28), calls=%async_computation.4 | async-start | bytes 32768 | tf_op jit(solution)/shard_map/all_to_all | solution.py:147
  51.4 11.0 %all-to-all-start = ((s32[8,3,8]{2,1,0:T(4,128)}), s32[8,3,8]{2,1,0:T(4,128)S(1)}, u32[]{:S(2)}, u32[]{:S(2)}) async-start(s32[8,3,8]{2,1,0:T(4,128)} %concatenate.24), calls=%async_computation | async-start | bytes 32768 | tf_op jit(solution)/shard_map/all_to_all | solution.py:147
  63.1 11.0 %all-to-all-start.6 = ((s32[8,3,8]{2,1,0:T(4,128)}), s32[8,3,8]{2,1,0:T(4,128)S(1)}, u32[]{:S(2)}, u32[]{:S(2)}) async-start(s32[8,3,8]{2,1,0:T(4,128)} %concatenate.30), calls=%async_computation.6 | async-start | bytes 32768 | tf_op jit(solution)/shard_map/all_to_all | solution.py:147
  101.6 30.9 %all-to-all-start.1 = ((bf16[8,1,2,2,128,128]{5,4,3,2,1,0:T(8,128)(2,1)}), bf16[8,1,2,2,128,128]{5,4,3,2,1,0:T(8,128)(2,1)S(1)}, u32[]{:S(2)}, u32[]{:S(2)}) async-start(bf16[8,1,2,2,128,128]{5,4,3,2,1,0:T(8,128)(2,1)} %bitcast_select_fusion.3), calls=%async_computation.1 | async-start | bytes 2097152 | tf_op jit(solution)/shard_map/all_to_all | solution.py:156
  132.5 7.4 %copy-start = (bf16[8,1,2,2,128,128]{5,4,3,2,1,0:T(8,128)(2,1)}, bf16[8,1,2,2,128,128]{5,4,3,2,1,0:T(8,128)(2,1)S(1)}, u32[]{:S(2)}) copy-start(bf16[8,1,2,2,128,128]{5,4,3,2,1,0:T(8,128)(2,1)S(1)} %all-to-all-done.1) | copy-start | bytes 3145732
  132.5 62.7 %all-to-all-start.3 = ((bf16[8,1,2,2,128,128]{5,4,3,2,1,0:T(8,128)(2,1)}), bf16[8,1,2,2,128,128]{5,4,3,2,1,0:T(8,128)(2,1)S(1)}, u32[]{:S(2)}, u32[]{:S(2)}) async-start(bf16[8,1,2,2,128,128]{5,4,3,2,1,0:T(8,128)(2,1)} %bitcast_select_fusion.2), calls=%async_computation.3 | async-start | bytes 2097152 | tf_op jit(solution)/shard_map/all_to_all | solution.py:156
  168.2 35.2 %collective-permute-start = (f32[8,2,128,128]{3,2,0,1:T(8,128)}, f32[8,2,128,128]{3,2,0,1:T(8,128)}, u32[]{:S(2)}, u32[]{:S(2)}) collective-permute-start(f32[8,2,128,128]{3,2,0,1:T(8,128)} %pad_maximum_fusion), channel_id=1, source_target_pairs={{0,8},{8,16},{16,24},{24,32},{32,40},{40,48},{48,56},{56,64},{64,7... | collective-permute-start | bytes 3145736 | tf_op jit(solution)/shard_map/ppermute | solution.py:14
  195.2 64.8 %all-to-all-start.5 = ((bf16[8,1,2,2,128,128]{5,4,3,2,1,0:T(8,128)(2,1)}), bf16[8,1,2,2,128,128]{5,4,3,2,1,0:T(8,128)(2,1)S(1)}, u32[]{:S(2)}, u32[]{:S(2)}) async-start(bf16[8,1,2,2,128,128]{5,4,3,2,1,0:T(8,128)(2,1)} %bitcast_select_fusion.1), calls=%async_computation.5 | async-start | bytes 2097152 | tf_op jit(solution)/shard_map/all_to_all | solution.py:156
  203.2 0.9 copy-start.1
  231.6 36.6 %collective-permute-start.1 = (f32[8,2,128,128]{3,2,0,1:T(8,128)}, f32[8,2,128,128]{3,2,0,1:T(8,128)}, u32[]{:S(2)}, u32[]{:S(2)}) collective-permute-start(f32[8,2,128,128]{3,2,0,1:T(8,128)} %pad_maximum_fusion.1), channel_id=1, source_target_pairs={{0,8},{8,16},{16,24},{24,32},{32,40},{40,48},{48,56},{56,64},{64,7... | collective-permute-start | bytes 3145736 | tf_op jit(solution)/shard_map/ppermute | solution.py:14
  260.0 37.2 %all-to-all-start.7 = ((bf16[8,1,2,2,128,128]{5,4,3,2,1,0:T(8,128)(2,1)}), bf16[8,1,2,2,128,128]{5,4,3,2,1,0:T(8,128)(2,1)S(1)}, u32[]{:S(2)}, u32[]{:S(2)}) async-start(bf16[8,1,2,2,128,128]{5,4,3,2,1,0:T(8,128)(2,1)} %bitcast_select_fusion), calls=%async_computation.7 | async-start | bytes 2097152 | tf_op jit(solution)/shard_map/all_to_all | solution.py:156
  294.8 18.3 %collective-permute-start.2 = (f32[8,2,128,128]{3,2,0,1:T(8,128)S(1)}, f32[8,2,128,128]{3,2,0,1:T(8,128)}, u32[]{:S(2)}, u32[]{:S(2)}) collective-permute-start(f32[8,2,128,128]{3,2,0,1:T(8,128)S(1)} %pad_maximum_fusion.2), channel_id=1, source_target_pairs={{0,8},{8,16},{16,24},{24,32},{32,40},{40,48},{48,56},{56,64},{64,7... | collective-permute-start | bytes 3145736 | tf_op jit(solution)/shard_map/ppermute | solution.py:14
